TPU v7x, 32 devices: a whole 2x2x4 slice. The times are simulated.
32 devices in a mesh: pipe: 1, expert: 32 (over z, y, x, core).
Axes of the slice: x: 2, y: 2, z: 4, core: 2. Of those that a mesh axis runs over, the one named last changes fastest.
Arguments:
- fwd_tokens: bfloat16 [1, 512, 3584], P('pipe', 'expert'), may hold values from -6 to 6
- fwd_routes: int32 [1, 512, 2], P('pipe', 'expert'), may hold values from 0 to 3, all different within a row; in each aligned block of 16 rows (0 to 15, 16 to 31, ..., all dimensions but the last counted through in order) at most 10 rows name the same one
- fwd_scores: float32 [1, 512, 2], P('pipe', 'expert'), may hold values from 0.1 to 1
- bwd_tokens: bfloat16 [1, 512, 3584], P('pipe', 'expert'), may hold values from -6 to 6
- bwd_routes: int32 [1, 512, 2], P('pipe', 'expert'), may hold values from 0 to 3, all different within a row; in each aligned block of 16 rows (0 to 15, 16 to 31, ..., all dimensions but the last counted through in order) at most 10 rows name the same one
- bwd_scores: float32 [1, 512, 2], P('pipe', 'expert'), may hold values from 0.1 to 1
- out_grad: bfloat16 [1, 512, 3584], P('pipe', 'expert'), may hold values from -6 to 6
- gate_weight: bfloat16 [1, 3584, 4096], P('pipe', None, 'expert'), may hold values from -0.09375 to 0.09375
- up_weight: bfloat16 [1, 3584, 4096], P('pipe', None, 'expert'), may hold values from -0.09375 to 0.09375
- down_weight: bfloat16 [1, 4096, 3584], P('pipe', 'expert'), may hold values from -0.1875 to 0.1875
Outputs:
- next_input: bfloat16 [1, 512, 3584], P('pipe', 'expert')
- prev_grad: bfloat16 [1, 512, 3584], P('pipe', 'expert')
Inputs may be any that keep to these rules, and one draw needn't show every extreme that they name: `fwd_routes`: each row names 2 different experts. Among the 16 rows of one device in one section, no expert is named more than 10 times, a bound that some block reaches. `bwd_routes`: each row names 2 different experts. Among the 16 rows of one device in one section, no expert is named more than 10 times, a bound that some block reaches.
All inputs are finite; a program needn't handle non-finite values.
Results may differ from a plain program's by a relative error of at most 0.011.
Values may be sent and summed in bfloat16 or wider, within the bound.
A program may use at most 128 MiB of HBM per device.

v0:
```python
import jax
import jax.numpy as jnp
from jax import lax
from jax.sharding import PartitionSpec as P

GROUP = 8


def from_behind(value, axis, steps):
    count = lax.axis_size(axis)
    pairs = [(source, (source + steps) % count) for source in range(count)]
    return lax.ppermute(value, axis, pairs)


def route_tables(routes, scores, capacity, experts):
    tokens, topk = routes.shape
    flat = routes.reshape(-1)
    onehot = (flat[:, None] == jnp.arange(experts, dtype=jnp.int32)[None, :]).astype(jnp.int32)
    rank = jnp.cumsum(onehot, axis=0) - onehot
    within = jnp.sum(rank * onehot, axis=1)
    slot_ids = (flat * capacity + within).reshape(tokens, topk)
    places = jnp.arange(experts * capacity, dtype=jnp.int32)
    hits = (slot_ids[:, :, None] == places[None, None, :]).astype(jnp.float32)
    normed = scores / jnp.sum(scores, axis=1, keepdims=True)
    member = jnp.sum(hits, axis=1)
    weighted = jnp.sum(hits * normed[:, :, None], axis=1)
    return (member, weighted)


def pick_rows(member, rows):
    slots = jnp.einsum(
        "te,td->ed", member.astype(jnp.bfloat16), rows, preferred_element_type=jnp.float32
    )
    return slots.astype(jnp.bfloat16)


def expert_forward(rows3, w_gate, w_up, w_down):
    width = rows3.shape[-1]
    flat = rows3.reshape(-1, width)
    first = jnp.dot(flat, w_gate, preferred_element_type=jnp.float32)
    second = jnp.dot(flat, w_up, preferred_element_type=jnp.float32)
    hidden = (jax.nn.silu(first) * second).astype(jnp.bfloat16)
    parts = jnp.dot(hidden, w_down, preferred_element_type=jnp.float32).astype(jnp.bfloat16)
    return parts.reshape(rows3.shape)


def expert_backward(rows3, grads3, w_gate, w_up, w_down):
    width = rows3.shape[-1]
    flat = rows3.reshape(-1, width)
    first = jnp.dot(flat, w_gate, preferred_element_type=jnp.float32)
    second = jnp.dot(flat, w_up, preferred_element_type=jnp.float32)
    d_hidden = lax.dot_general(
        grads3.reshape(-1, width),
        w_down,
        (((1,), (1,)), ((), ())),
        preferred_element_type=jnp.float32,
    )
    sigm = 1.0 / (1.0 + jnp.exp(-first))
    d_first = (d_hidden * second * sigm * (1.0 + first * (1.0 - sigm))).astype(jnp.bfloat16)
    d_second = (d_hidden * first * sigm).astype(jnp.bfloat16)
    back = lax.dot_general(
        d_first, w_gate, (((1,), (1,)), ((), ())), preferred_element_type=jnp.float32
    )
    back = back + lax.dot_general(
        d_second, w_up, (((1,), (1,)), ((), ())), preferred_element_type=jnp.float32
    )
    return back.astype(jnp.bfloat16).reshape(rows3.shape)


def expert_work(arrived, weights):
    w_gate, w_up, w_down = weights
    kinds = arrived.shape[0]
    if kinds == 1:
        return expert_forward(arrived[0], w_gate, w_up, w_down)[None]
    return expert_backward(arrived[0], arrived[1], w_gate, w_up, w_down)[None]


def pass_rows(payload, weights):
    kinds, experts, capacity, width = payload.shape
    spread = jnp.broadcast_to(payload[:, :, None], (kinds, experts, GROUP, capacity, width))
    spread = spread.reshape(kinds, experts * GROUP, capacity, width)
    returned = lax.all_to_all(
        expert_work(
            lax.all_to_all(spread, "expert", split_axis=1, concat_axis=1, tiled=True), weights
        ),
        "expert",
        split_axis=1,
        concat_axis=1,
        tiled=True,
    )
    outkinds = returned.shape[0]
    summed = jnp.sum(
        returned.reshape(outkinds, experts, GROUP, capacity, width).astype(jnp.float32), axis=2
    )
    return summed.reshape(outkinds, experts * capacity, width)


def body(
    fwd_tokens,
    fwd_routes,
    fwd_scores,
    bwd_tokens,
    bwd_routes,
    bwd_scores,
    out_grad,
    gate_weight,
    up_weight,
    down_weight,
):
    experts = lax.axis_size("expert") // GROUP
    tokens = fwd_tokens.shape[1]
    topk = fwd_routes.shape[2]
    width = fwd_tokens.shape[2]
    capacity = min(tokens, max(6, (tokens * topk + experts - 1) // experts + 2))
    weights = (gate_weight[0], up_weight[0], down_weight[0])
    member_f, weight_f = route_tables(fwd_routes[0], fwd_scores[0], capacity, experts)
    member_b, weight_b = route_tables(bwd_routes[0], bwd_scores[0], capacity, experts)
    send_f = pick_rows(member_f, fwd_tokens[0]).reshape(experts, capacity, width)
    send_x = pick_rows(member_b, bwd_tokens[0]).reshape(experts, capacity, width)
    route_grad = jnp.einsum(
        "te,td->ed", weight_b, out_grad[0].astype(jnp.float32), precision=lax.Precision.HIGHEST
    )
    send_g = route_grad.astype(jnp.bfloat16).reshape(experts, capacity, width)
    sum_f = pass_rows(send_f[None], weights)[0]
    sum_b = pass_rows(jnp.stack((send_x, send_g)), weights)[0]
    layer_out = jnp.dot(weight_f, sum_f, precision=lax.Precision.HIGHEST).astype(jnp.bfloat16)[None]
    input_grad = jnp.dot(member_b, sum_b, precision=lax.Precision.HIGHEST).astype(jnp.bfloat16)[
        None
    ]
    next_input = from_behind(layer_out, "pipe", 1)
    prev_grad = from_behind(input_grad, "pipe", -1)
    return (next_input, prev_grad)


def solution(mesh):
    placed = (
        P("pipe", "expert", None),
        P("pipe", "expert", None),
        P("pipe", "expert", None),
        P("pipe", "expert", None),
        P("pipe", "expert", None),
        P("pipe", "expert", None),
        P("pipe", "expert", None),
        P("pipe", None, "expert"),
        P("pipe", None, "expert"),
        P("pipe", "expert", None),
    )
    return jax.shard_map(
        body,
        mesh=mesh,
        in_specs=placed,
        out_specs=(P("pipe", "expert", None), P("pipe", "expert", None)),
        check_vma=False,
    )
```

profile of v0, /device:TPU:0, one launch (start us, length us, event | category | flops | bytes accessed | tf_op | source)
XLA Modules:
  0.0 386.7 jit_solution(8112872531019450268)
XLA Ops:
  0.6 0.8 copy.39
  1.5 0.1 eq.56
  1.7 0.2 select_reduce_fusion.3
  2.0 0.1 copy.40
  2.1 0.7 bitcast_add_fusion.1
  2.8 0.7 reduce_sum.96
  3.5 0.7 bitcast_divide_fusion.1
  4.2 1.2 convolution_convert_fusion.3
  5.4 0.1 broadcast_in_dim.12
  5.5 2.3 broadcast_in_dim.13
  7.7 7.4 %all-to-all-start = ((bf16[1,32,10,3584]{3,2,0,1:T(8,128)(2,1)}), bf16[1,32,10,3584]{3,2,0,1:T(8,128)(2,1)}, u32[]{:S(2)}, u32[]{:S(2)}) async-start(bf16[1,32,10,3584]{3,2,0,1:T(8,128)(2,1)} %bitcast.64), calls=%async_computation | async-start | bytes 7340032 | tf_op jit(solution)/shard_map/all_to_all | solution.py:84
  15.3 0.1 eq.63
  15.5 0.2 select_reduce_fusion.1
  15.8 0.1 copy.43
  16.0 0.3 convolution_convert_fusion.2
  16.2 0.1 stack_reshape.6
  16.4 0.4 convolution_convert_fusion.1
  16.8 0.1 stack_reshape.7
  16.9 0.1 pad_maximum_fusion
  17.0 0.6 copy.44
  17.6 80.2 %all-to-all-done = bf16[1,32,10,3584]{3,2,0,1:T(8,128)(2,1)} async-done(((bf16[1,32,10,3584]{3,2,0,1:T(8,128)(2,1)}), bf16[1,32,10,3584]{3,2,0,1:T(8,128)(2,1)}, u32[]{:S(2)}, u32[]{:S(2)}) %all-to-all-start) | async-done | bytes 2293792 | tf_op jit(solution)/shard_map/all_to_all | solution.py:84
  97.8 4.4 %broadcast_in_dim.16 = bf16[2,4,8,10,3584]{4,0,3,2,1:T(2,128)(2,1)} broadcast(bf16[2,4,10,3584]{3,0,2,1:T(2,128)(2,1)S(1)} %copy.44), dimensions={0,1,3,4} | broadcast | bytes 5160960 | tf_op jit(solution)/shard_map/broadcast_in_dim | solution.py:80
  102.2 4.1 %all-to-all-start.2 = ((bf16[2,32,10,3584]{3,0,2,1:T(2,128)(2,1)}), bf16[2,32,10,3584]{3,0,2,1:T(2,128)(2,1)}, u32[]{:S(2)}, u32[]{:S(2)}) async-start(bf16[2,32,10,3584]{3,0,2,1:T(2,128)(2,1)} %bitcast.63), calls=%async_computation.2 | async-start | bytes 9175040 | tf_op jit(solution)/shard_map/all_to_all | solution.py:84
  106.3 3.1 reshape_squeeze.11
  109.5 1.9 fusion.19
  111.4 5.1 %convolution_convert_fusion = bf16[320,3584]{1,0:T(8,128)(2,1)} fusion(bf16[320,3584]{1,0:T(8,128)(2,1)S(1)} %reshape_squeeze.11, bf16[1,128,3584]{2,1,0:T(8,128)(2,1)} %param.19, bf16[1,3584,128]{2,1,0:T(8,128)(2,1)S(1)} %copy-done, f32[320,128]{1,0:T(8,128)S(1)} %fusion.19), kind=kOutput, calls=%fused_computation.4 | convolution fusion | flops 588595200 | bytes 6586368 | tf_op jit(solution)/shard_map/dot_general | solution.py:43
  116.5 4.4 %broadcast_in_dim_reshape.8 = bf16[1,32,10,3584]{3,2,1,0:T(8,128)(2,1)} reshape(bf16[320,3584]{1,0:T(8,128)(2,1)} %convolution_convert_fusion) | data formatting | bytes 4587520 | tf_op jit(solution)/shard_map/broadcast_in_dim;reshape | solution.py:74
  121.0 87.8 %all-to-all-done.2 = bf16[2,32,10,3584]{3,0,2,1:T(2,128)(2,1)} async-done(((bf16[2,32,10,3584]{3,0,2,1:T(2,128)(2,1)}), bf16[2,32,10,3584]{3,0,2,1:T(2,128)(2,1)}, u32[]{:S(2)}, u32[]{:S(2)}) %all-to-all-start.2) | async-done | bytes 4587552 | tf_op jit(solution)/shard_map/all_to_all | solution.py:84
  208.8 4.1 %all-to-all-start.1 = ((bf16[1,32,10,3584]{3,2,0,1:T(8,128)(2,1)}), bf16[1,32,10,3584]{3,2,0,1:T(8,128)(2,1)}, u32[]{:S(2)}, u32[]{:S(2)}) async-start(bf16[1,32,10,3584]{3,2,0,1:T(8,128)(2,1)} %bitcast.65), calls=%async_computation.1 | async-start | bytes 7340032 | tf_op jit(solution)/shard_map/all_to_all | solution.py:82
  212.9 25.0 %slice_reduce_fusion = (bf16[32,10,3584]{2,1,0:T(8,128)(2,1)}, bf16[32,10,3584]{2,1,0:T(8,128)(2,1)}) fusion(bf16[2,32,10,3584]{3,0,2,1:T(2,128)(2,1)} %all-to-all-done.2), kind=kLoop, calls=%fused_computation.5 | loop fusion | bytes 9175040 | tf_op jit(solution)/shard_map/slice | solution.py:75
  237.9 3.1 reshape_squeeze.13
  241.0 4.5 %reshape_squeeze.12 = bf16[320,3584]{1,0:T(8,128)(2,1)} reshape(bf16[32,10,3584]{2,1,0:T(8,128)(2,1)} %get-tuple-element.3) | data formatting | bytes 4587520 | tf_op jit(solution)/shard_map/reshape;squeeze | solution.py:53
  245.5 2.1 fusion.17
  247.6 0.7 fusion.8
  248.4 5.9 %fusion.7 = f32[320,3584]{1,0:T(8,128)} fusion(f32[320,128]{1,0:T(8,128)S(1)} %fusion.8, bf16[320,3584]{1,0:T(8,128)(2,1)S(1)} %reshape_squeeze.13, bf16[1,3584,128]{2,1,0:T(8,128)(2,1)S(1)} %copy-done, bf16[1,3584,128]{2,1,0:T(8,128)(2,1)} %param.17, f32[320,128]{1,0:T(8,128)S(1)} %fusion.17), kind=kOutput, calls=%fused_computation.20 | convolution fusion | flops 587612160 | bytes 9043968 | tf_op jit(solution)/shard_map/dot_general | solution.py:61
  254.3 3.1 fusion
  257.4 2.7 broadcast_in_dim_reshape.9
  260.1 35.4 %all-to-all-done.1 = bf16[1,32,10,3584]{3,2,0,1:T(8,128)(2,1)} async-done(((bf16[1,32,10,3584]{3,2,0,1:T(8,128)(2,1)}), bf16[1,32,10,3584]{3,2,0,1:T(8,128)(2,1)}, u32[]{:S(2)}, u32[]{:S(2)}) %all-to-all-start.1) | async-done | bytes 2293792 | tf_op jit(solution)/shard_map/all_to_all | solution.py:82
  295.5 4.0 %all-to-all-start.3 = ((bf16[1,32,10,3584]{3,2,0,1:T(8,128)(2,1)}), bf16[1,32,10,3584]{3,2,0,1:T(8,128)(2,1)}, u32[]{:S(2)}, u32[]{:S(2)}) async-start(bf16[1,32,10,3584]{3,2,0,1:T(8,128)(2,1)} %bitcast.66), calls=%async_computation.3 | async-start | bytes 7340032 | tf_op jit(solution)/shard_map/all_to_all | solution.py:82
  299.5 2.7 convert_reduce_fusion.1
  302.2 0.1 squeeze_reshape.6
  302.3 0.4 fusion.1
  302.7 79.4 %all-to-all-done.3 = bf16[1,32,10,3584]{3,2,0,1:T(8,128)(2,1)} async-done(((bf16[1,32,10,3584]{3,2,0,1:T(8,128)(2,1)}), bf16[1,32,10,3584]{3,2,0,1:T(8,128)(2,1)}, u32[]{:S(2)}, u32[]{:S(2)}) %all-to-all-start.3) | async-done | bytes 2293792 | tf_op jit(solution)/shard_map/all_to_all | solution.py:82
  382.1 2.7 convert_reduce_fusion
  384.9 0.1 squeeze_reshape.7
  384.9 0.4 fusion.2
  385.4 0.6 copy.50
  386.0 0.6 copy.51
  (30 shorter events, 0.8 us)
Async XLA Ops:
  0.6 110.8 %copy-start = (bf16[1,3584,128]{2,1,0:T(8,128)(2,1)S(1)}, bf16[1,3584,128]{2,1,0:T(8,128)(2,1)}, u32[]{:S(2)}) copy-start(bf16[1,3584,128]{2,1,0:T(8,128)(2,1)} %param.18) | copy-start | bytes 2752516
  7.7 7.4 %copy-start.5 = (s32[1,16,2]{1,2,0:T(2,128)S(1)}, s32[1,16,2]{1,2,0:T(2,128)}, u32[]{:S(2)}) copy-start(s32[1,16,2]{1,2,0:T(2,128)} %param.14) | copy-start | bytes 388
  7.7 8.1 %copy-start.6 = (f32[1,16,2]{1,2,0:T(2,128)S(1)}, f32[1,16,2]{1,2,0:T(2,128)}, u32[]{:S(2)}) copy-start(f32[1,16,2]{1,2,0:T(2,128)} %param.15) | copy-start | bytes 388
  7.7 8.2 %copy-start.3 = (bf16[1,16,3584]{2,1,0:T(8,128)(2,1)S(1)}, bf16[1,16,3584]{2,1,0:T(8,128)(2,1)}, u32[]{:S(2)}) copy-start(bf16[1,16,3584]{2,1,0:T(8,128)(2,1)} %param.13) | copy-start | bytes 344068
  7.7 8.6 %copy-start.4 = (bf16[1,16,3584]{2,1,0:T(8,128)(2,1)S(1)}, bf16[1,16,3584]{2,1,0:T(8,128)(2,1)}, u32[]{:S(2)}) copy-start(bf16[1,16,3584]{2,1,0:T(8,128)(2,1)} %param.16) | copy-start | bytes 344068
  7.7 90.1 %all-to-all-start = ((bf16[1,32,10,3584]{3,2,0,1:T(8,128)(2,1)}), bf16[1,32,10,3584]{3,2,0,1:T(8,128)(2,1)}, u32[]{:S(2)}, u32[]{:S(2)}) async-start(bf16[1,32,10,3584]{3,2,0,1:T(8,128)(2,1)} %bitcast.64), calls=%async_computation | async-start | bytes 7340032 | tf_op jit(solution)/shard_map/all_to_all | solution.py:84
  102.2 106.5 %all-to-all-start.2 = ((bf16[2,32,10,3584]{3,0,2,1:T(2,128)(2,1)}), bf16[2,32,10,3584]{3,0,2,1:T(2,128)(2,1)}, u32[]{:S(2)}, u32[]{:S(2)}) async-start(bf16[2,32,10,3584]{3,0,2,1:T(2,128)(2,1)} %bitcast.63), calls=%async_computation.2 | async-start | bytes 9175040 | tf_op jit(solution)/shard_map/all_to_all | solution.py:84
  208.8 86.7 %all-to-all-start.1 = ((bf16[1,32,10,3584]{3,2,0,1:T(8,128)(2,1)}), bf16[1,32,10,3584]{3,2,0,1:T(8,128)(2,1)}, u32[]{:S(2)}, u32[]{:S(2)}) async-start(bf16[1,32,10,3584]{3,2,0,1:T(8,128)(2,1)} %bitcast.65), calls=%async_computation.1 | async-start | bytes 7340032 | tf_op jit(solution)/shard_map/all_to_all | solution.py:82
  245.5 2.1 copy-start.1
  245.5 2.1 copy-start.2
  295.5 86.6 %all-to-all-start.3 = ((bf16[1,32,10,3584]{3,2,0,1:T(8,128)(2,1)}), bf16[1,32,10,3584]{3,2,0,1:T(8,128)(2,1)}, u32[]{:S(2)}, u32[]{:S(2)}) async-start(bf16[1,32,10,3584]{3,2,0,1:T(8,128)(2,1)} %bitcast.66), calls=%async_computation.3 | async-start | bytes 7340032 | tf_op jit(solution)/shard_map/all_to_all | solution.py:82
  302.7 82.7 %collective-permute-start = (bf16[1,16,3584]{2,1,0:T(8,128)(2,1)S(1)}, bf16[1,16,3584]{2,1,0:T(8,128)(2,1)S(1)}, u32[]{:S(2)}, u32[]{:S(2)}) collective-permute-start(bf16[1,16,3584]{2,1,0:T(8,128)(2,1)S(1)} %fusion.1), channel_id=1, source_target_pairs={{0,0},{1,1},{2,2},{3,3},{4,4},{5,5},{6,6},{7,7},{8,8},{9,9},{10,10... | collective-permute-start | bytes 344072 | tf_op jit(solution)/shard_map/ppermute | solution.py:12
  (1 other events, 0.0 us)
where the time goes:
time: 388 us; the launch traced here: 387 us
  waiting for transfers between devices  283 us (73%)
  local copies, waits for them, and re-layouts  53.3 us (14%)
  matrix products  21.5 us (6%)
  starting transfers between devices  19.6 us (5%)
  other arithmetic  8.5 us (2%)
    all_to_all x2, waiting for transfers between devices, pass_rows(): lax.all_to_all(spread, 'expert', split_axis=1, concat_axis=1, tiled=True)  168 us
    all_to_all x2, waiting for transfers between devices, pass_rows(): lax.all_to_all(expert_work(lax.all_to_all(spread, 'expert', split_axis=1,...  115 us
    slice x1, local copies, waits for them, and re-layouts, expert_work(): return expert_backward(arrived[0], arrived[1], w_gate, w_up, w_down)[None]  25 us
    all_to_all x2, starting transfers between devices, pass_rows(): lax.all_to_all(spread, 'expert', split_axis=1, concat_axis=1, tiled=True)  11.5 us
    all_to_all x2, starting transfers between devices, pass_rows(): lax.all_to_all(expert_work(lax.all_to_all(spread, 'expert', split_axis=1,...  8.11 us
  transfers between devices with their start and end apart: 6, of which 4 were waited for; matrix products, arithmetic and copies ran while one was open for 18% of the time, Pallas kernels for 0%

commit v1 on v0

v1 whole, which is shorter than its diff:
```python
import functools

import jax
import jax.numpy as jnp
from jax import lax
from jax.experimental import pallas as pl
from jax.experimental.pallas import tpu as pltpu
from jax.sharding import PartitionSpec as P

GROUP = 8
CHUNKS = 4
F32 = jnp.float32
BF16 = jnp.bfloat16


def flip(value, mask):
    out, bit = value, 1
    while bit <= mask:
        if mask & bit:
            out = out + bit - 2 * bit * (lax.div(value, bit) % 2)
        bit *= 2
    return out


def nt(a, b):
    return lax.dot_general(a, b, (((1,), (1,)), ((), ())), preferred_element_type=F32)


def nn(a, b):
    return jnp.dot(a, b, preferred_element_type=F32)


def kernel(
    experts, cap, slot, chunks,
    info, info_t, tok_f, tok_b, grad, wg, wu, wd, y_ref, dx_ref,
    bundles, gathered, acc, hidden, away, near, from_pair, summed, diag, relay,
    from_x, from_y, back, home,
    z_s, z_r, own_s, own_r, dia_s, dia_r, pair_s, pair_r,
    op_s, op_r, dg_s, dg_r, x_s, x_r, y_s, y_r, b_s, b_r,
):
    tokens, width = tok_f.shape
    cols = width // chunks
    rows = experts * slot
    live = 2 * cap
    outs = experts * live
    me = lax.axis_index("expert")
    mine = lax.div(me, GROUP)
    pair, chip_x, chip_y = flip(me, 1), flip(me, 2), flip(me, 4)
    planes = [None] + [flip(mine, d) * GROUP + lax.rem(me, GROUP) for d in range(1, experts)]

    def copy(src, dst, send, recv, target):
        return pltpu.make_async_remote_copy(
            src_ref=src, dst_ref=dst, send_sem=send, recv_sem=recv,
            device_id={"expert": target}, device_id_type=pl.DeviceIdType.MESH,
        )

    def z_copy(c, d):
        return copy(bundles.at[c, d], gathered.at[c, 0, d], z_s.at[c, d], z_r.at[c, d], planes[d])

    def own_copy(c, k):
        return copy(gathered.at[c, 0], gathered.at[c, k], own_s.at[c, k], own_r.at[c, k],
                    chip_x if k == 1 else chip_y)

    def dia_copy(c):
        k, target = (1, chip_y) if c % 2 == 0 else (2, chip_x)
        return copy(gathered.at[c, k], gathered.at[c, 3], dia_s.at[c], dia_r.at[c], target)

    def pair_copy(c, k):
        return copy(gathered.at[c, k], gathered.at[c, 4 + k], pair_s.at[c, k], pair_r.at[c, k], pair)

    def op_copy(c):
        return copy(away.at[c], from_pair.at[c], op_s.at[c], op_r.at[c], pair)

    def dg_copy(c):
        return copy(summed.at[c, 3], diag.at[c], dg_s.at[c], dg_r.at[c],
                    chip_x if c % 2 == 0 else chip_y)

    def x_copy(c):
        src = summed.at[c, 1] if c % 2 == 0 else relay.at[c]
        return copy(src, from_x.at[c], x_s.at[c], x_r.at[c], chip_x)

    def y_copy(c):
        src = relay.at[c] if c % 2 == 0 else summed.at[c, 2]
        return copy(src, from_y.at[c], y_s.at[c], y_r.at[c], chip_y)

    def b_copy(c, d):
        return copy(back.at[c, d], home.at[c, d], b_s.at[c, d], b_r.at[c, d], planes[d])

    barrier = pltpu.get_barrier_semaphore()
    friends = [pair, chip_x, chip_y] + planes[1:]
    for friend in friends:
        pl.semaphore_signal(barrier, inc=1, device_id={"expert": friend},
                            device_id_type=pl.DeviceIdType.MESH)

    first = lax.broadcasted_iota(jnp.int32, (tokens, tokens), 0)
    second = lax.broadcasted_iota(jnp.int32, (tokens, tokens), 1)
    up = (first < second).astype(F32)
    low = (second < first).astype(F32)
    place_r = lax.broadcasted_iota(jnp.int32, (rows, tokens), 0).astype(F32)
    place_c = lax.broadcasted_iota(jnp.int32, (tokens, rows), 1).astype(F32)
    pick_f = jnp.zeros((rows, tokens), F32)
    pick_x = jnp.zeros((rows, tokens), F32)
    pick_g = jnp.zeros((rows, tokens), F32)
    gain = jnp.zeros((rows, 1), F32)
    join_f = jnp.zeros((tokens, rows), F32)
    join_b = jnp.zeros((tokens, rows), F32)
    norm_r = info_t[6:7, :] + info_t[7:8, :]
    norm_c = info[:, 4:5] + info[:, 5:6]
    for d in range(experts):
        want = flip(mine, d).astype(F32)
        for b in (0, 2):
            row0, row1 = info_t[b:b + 1, :] == want, info_t[b + 1:b + 2, :] == want
            col0, col1 = info[:, b:b + 1] == want, info[:, b + 1:b + 2] == want
            in_row = row0 | row1
            in_col = col0 | col1
            rank_r = jnp.sum(jnp.where(in_col, up, 0.0), axis=0, keepdims=True)
            rank_c = jnp.sum(jnp.where(in_row, low, 0.0), axis=1, keepdims=True)
            rank_r = jnp.where(in_row, rank_r, -1e6) + float(d * slot)
            rank_c = jnp.where(in_col, rank_c, -1e6) + float(d * slot)
            if b == 0:
                pick_f = pick_f + (place_r == rank_r).astype(F32)
                weight = jnp.where(col0, info[:, 4:5], info[:, 5:6]) / norm_c
                join_f = join_f + jnp.where(place_c == rank_c, weight, 0.0)
            else:
                pick_x = pick_x + (place_r == rank_r + cap).astype(F32)
                hit = place_r == rank_r + 2 * cap
                pick_g = pick_g + hit.astype(F32)
                weight = jnp.where(row0, info_t[6:7, :], info_t[7:8, :]) / norm_r
                gain = gain + jnp.sum(jnp.where(hit, weight, 0.0), axis=1, keepdims=True)
                join_b = join_b + (place_c == rank_c + cap).astype(F32)
    pick_f, pick_x, pick_g = pick_f.astype(BF16), pick_x.astype(BF16), pick_g.astype(BF16)
    high = join_f.astype(BF16)
    rest = join_f - high.astype(F32)
    middle = rest.astype(BF16)
    last = (rest - middle.astype(F32)).astype(BF16)
    join = jnp.concatenate([high, middle, last, join_b.astype(BF16)], axis=0)

    pl.semaphore_wait(barrier, len(friends))
    for c in range(chunks):
        at = slice(c * cols, (c + 1) * cols)
        block = nn(pick_f, tok_f[:, at]) + nn(pick_x, tok_b[:, at]) + gain * nn(pick_g, grad[:, at])
        block = block.astype(BF16).reshape(experts, slot, cols)
        gathered[c, 0, 0] = block[0]
        for d in range(1, experts):
            bundles[c, d] = block[d]
            z_copy(c, d).start()

    acc[...] = jnp.zeros_like(acc)

    def gather_own(c):
        for d in range(1, experts):
            z_copy(c, d).wait_recv()
        own_copy(c, 1).start()
        own_copy(c, 2).start()
        pair_copy(c, 0).start()

    def gather_next(c):
        order = (1, 2) if c % 2 == 0 else (2, 1)
        own_copy(c, order[0]).wait_recv()
        dia_copy(c).start()
        pair_copy(c, order[0]).start()
        own_copy(c, order[1]).wait_recv()
        pair_copy(c, order[1]).start()

    def gather_last(c):
        dia_copy(c).wait_recv()
        pair_copy(c, 3).start()

    def multiply(c):
        for k in range(4):
            pair_copy(c, k).wait_recv()
        at = slice(c * cols, (c + 1) * cols)

        def one(q, carry):
            part = gathered[c, q].reshape(rows, cols)
            acc[q, :, 0:128] += nn(part, wg[at, :])
            acc[q, :, 128:256] += nn(part, wu[at, :])
            acc[q, :, 256:384] += nt(part, wd[:, at])
            return carry

        lax.fori_loop(0, 8, one, 0)

    for step in range(chunks + 3):
        for lag, stage in enumerate((gather_own, gather_next, gather_last, multiply)):
            if 0 <= step - lag < chunks:
                stage(step - lag)

    out_i = lax.broadcasted_iota(jnp.int32, (outs, rows), 0)
    in_i = lax.broadcasted_iota(jnp.int32, (outs, rows), 1)
    squeeze = jnp.zeros((outs, rows), F32)
    out_t = lax.broadcasted_iota(jnp.int32, (rows, outs), 1)
    in_t = lax.broadcasted_iota(jnp.int32, (rows, outs), 0)
    spread = jnp.zeros((rows, outs), F32)
    for d in range(experts):
        shift = d * (slot - live)
        squeeze = squeeze + ((in_i == out_i + shift) & (out_i >= d * live) & (out_i < (d + 1) * live)).astype(F32)
        spread = spread + ((in_t == out_t + shift) & (out_t >= d * live) & (out_t < (d + 1) * live)).astype(F32)
    squeeze, spread = squeeze.astype(BF16), spread.astype(BF16)
    place = lax.broadcasted_iota(jnp.int32, (rows, 128), 0) % slot
    is_f = place < cap
    is_x = (place >= cap) & (place < 2 * cap)

    def activate(q, carry):
        a, b = acc[q, :, 0:128], acc[q, :, 128:256]
        dh = pltpu.roll(acc[q, :, 256:384], rows - cap, 0)
        sg = 1.0 / (1.0 + jnp.exp(-a))
        h = jnp.where(is_f, a * sg * b, 0.0).astype(BF16)
        da = jnp.where(is_x, dh * b * sg * (1.0 + a * (1.0 - sg)), 0.0).astype(BF16)
        db = jnp.where(is_x, dh * a * sg, 0.0).astype(BF16)
        hidden[q, :, 0:128] = nn(squeeze, h).astype(BF16)
        hidden[q, :, 128:256] = nn(squeeze, da).astype(BF16)
        hidden[q, :, 256:384] = nn(squeeze, db).astype(BF16)
        return carry

    lax.fori_loop(0, 8, activate, 0)

    def partial(q, c):
        at = slice(c * cols, (c + 1) * cols)
        total = nn(hidden[q, :, 0:128], wd[:, at])
        total = total + nt(hidden[q, :, 128:256], wg[at, :])
        total = total + nt(hidden[q, :, 256:384], wu[at, :])
        return total.astype(BF16)

    def produce(c):
        def far(r, carry):
            away[c, r] = partial(4 + r, c)
            return carry

        def close(r, carry):
            near[c, r] = partial(r, c)
            return carry

        lax.fori_loop(0, 4, far, 0)
        op_copy(c).start()
        lax.fori_loop(0, 4, close, 0)

    def chip_sum(c):
        op_copy(c).wait_recv()

        def add(r, carry):
            summed[c, r] = (near[c, r].astype(F32) + from_pair[c, r].astype(F32)).astype(BF16)
            return carry

        lax.fori_loop(0, 4, add, 0)
        dg_copy(c).start()
        if c % 2 == 0:
            x_copy(c).start()
        else:
            y_copy(c).start()

    def pass_on(c):
        dg_copy(c).wait_recv()
        k = 2 if c % 2 == 0 else 1
        relay[c] = (summed[c, k].astype(F32) + diag[c].astype(F32)).astype(BF16)
        if c % 2 == 0:
            y_copy(c).start()
        else:
            x_copy(c).start()

    def give_back(c):
        x_copy(c).wait_recv()
        y_copy(c).wait_recv()
        total = summed[c, 0].astype(F32) + from_x[c].astype(F32) + from_y[c].astype(F32)
        wide = nn(spread, total.astype(BF16)).astype(BF16).reshape(experts, slot, cols)
        home[c, 0] = wide[0]
        for d in range(1, experts):
            back[c, d] = wide[d]
            b_copy(c, d).start()

    def finish(c):
        for d in range(1, experts):
            b_copy(c, d).wait_recv()
        at = slice(c * cols, (c + 1) * cols)
        got = nn(join, home[c].reshape(rows, cols))
        t = tokens
        y_ref[:, at] = (got[0:t] + got[t:2 * t] + got[2 * t:3 * t]).astype(BF16)
        dx_ref[:, at] = got[3 * t:4 * t].astype(BF16)

    for step in range(chunks + 4):
        for lag, stage in enumerate((produce, chip_sum, pass_on, give_back, finish)):
            if 0 <= step - lag < chunks:
                stage(step - lag)

    for c in range(chunks):
        for d in range(1, experts):
            z_copy(c, d).wait_send()
            b_copy(c, d).wait_send()
        for k in (1, 2):
            own_copy(c, k).wait_send()
        for k in range(4):
            pair_copy(c, k).wait_send()
        for made in (dia_copy, op_copy, dg_copy, x_copy, y_copy):
            made(c).wait_send()


def body(
    fwd_tokens, fwd_routes, fwd_scores, bwd_tokens, bwd_routes, bwd_scores,
    out_grad, gate_weight, up_weight, down_weight,
):
    experts = lax.axis_size("expert") // GROUP
    tokens, width = fwd_tokens.shape[1:]
    topk = fwd_routes.shape[2]
    cap = min(tokens, max(6, (tokens * topk + experts - 1) // experts + 2))
    slot = -(-3 * cap // 16) * 16
    rows, outs = experts * slot, experts * 2 * cap
    chunks = CHUNKS
    cols = width // chunks
    info = jnp.concatenate(
        [fwd_routes[0].astype(F32), bwd_routes[0].astype(F32), fwd_scores[0], bwd_scores[0]], axis=1
    )
    dma = pltpu.SemaphoreType.DMA
    vmem = lambda *shape: pltpu.VMEM(shape, BF16)
    y, dx = pl.pallas_call(
        functools.partial(kernel, experts, cap, slot, chunks),
        out_shape=[jax.ShapeDtypeStruct((tokens, width), BF16)] * 2,
        in_specs=[pl.BlockSpec(memory_space=pltpu.VMEM)] * 8,
        out_specs=[pl.BlockSpec(memory_space=pltpu.VMEM)] * 2,
        scratch_shapes=[
            vmem(chunks, experts, slot, cols),
            vmem(chunks, 8, experts, slot, cols),
            pltpu.VMEM((8, rows, 384), F32),
            vmem(8, outs, 384),
            vmem(chunks, 4, outs, cols),
            vmem(chunks, 4, outs, cols),
            vmem(chunks, 4, outs, cols),
            vmem(chunks, 4, outs, cols),
            vmem(chunks, outs, cols),
            vmem(chunks, outs, cols),
            vmem(chunks, outs, cols),
            vmem(chunks, outs, cols),
            vmem(chunks, experts, slot, cols),
            vmem(chunks, experts, slot, cols),
            dma((chunks, experts)), dma((chunks, experts)),
            dma((chunks, 3)), dma((chunks, 3)),
            dma((chunks,)), dma((chunks,)),
            dma((chunks, 4)), dma((chunks, 4)),
            dma((chunks,)), dma((chunks,)),
            dma((chunks,)), dma((chunks,)),
            dma((chunks,)), dma((chunks,)),
            dma((chunks,)), dma((chunks,)),
            dma((chunks, experts)), dma((chunks, experts)),
        ],
        compiler_params=pltpu.CompilerParams(
            collective_id=0, has_side_effects=True, vmem_limit_bytes=58 * 1024 * 1024
        ),
    )(info, info.T, fwd_tokens[0], bwd_tokens[0], out_grad[0],
      gate_weight[0], up_weight[0], down_weight[0])
    y, dx = y[None], dx[None]
    count = lax.axis_size("pipe")
    if count > 1:
        y = lax.ppermute(y, "pipe", [(s, (s + 1) % count) for s in range(count)])
        dx = lax.ppermute(dx, "pipe", [(s, (s - 1) % count) for s in range(count)])
    return (y, dx)


def solution(mesh):
    row = P("pipe", "expert", None)
    placed = (row,) * 7 + (P("pipe", None, "expert"), P("pipe", None, "expert"), row)
    return jax.shard_map(
        body, mesh=mesh, in_specs=placed, out_specs=(row, row), check_vma=False
    )
```

time: 388 us -> 102 us (0.26)
  waiting for transfers between devices: 283 us -> 0 us
  Pallas kernels: 0 us -> 95.8 us
  local copies, waits for them, and re-layouts: 53.3 us -> 4.28 us
  matrix products: 21.5 us -> 0 us
  starting transfers between devices: 19.6 us -> 0 us
  other arithmetic: 8.5 us -> 0.6 us
    all_to_all x4 -> x0, waiting for transfers between devices: 283 us -> none  [the longest x2 168 us: pass_rows(): lax.all_to_all(spread, 'expert', split_axis=1, concat_axis=1, tiled=True)]
    pallas_call x0 -> x1, Pallas kernels: none -> 95.8 us  [body(): pl.pallas_call(functools.partial(kernel, experts, cap, slot, chunks), out...]
    slice x1 -> x0, local copies, waits for them, and re-layouts: 25 us -> none  [expert_work(): return expert_backward(arrived[0], arrived[1], w_gate, w_up, w_down)[None]]
    dot_general x11 -> x0, matrix products: 21.5 us -> none  [the longest x1 5.92 us: expert_backward(): lax.dot_general(d_first, w_gate, (((1,), (1,)), ((), ())), preferred_elem...]
    all_to_all x4 -> x0, starting transfers between devices: 19.6 us -> none  [the longest x2 11.5 us: pass_rows(): lax.all_to_all(spread, 'expert', split_axis=1, concat_axis=1, tiled=True)]
    another operation x10 -> x0, local copies, waits for them, and re-layouts: 18.8 us -> none  [the longest x1 4.49 us: expert_backward(): grads3.reshape(-1, width)]
    broadcast_in_dim x3 -> x0, local copies, waits for them, and re-layouts: 6.79 us -> none  [pass_rows(): jnp.broadcast_to(payload[:, :, None], (kinds, experts, GROUP, capacity, w...]
    reduce_sum x8 -> x0, other arithmetic: 6.73 us -> none  [the longest x2 5.49 us: pass_rows(): jnp.sum(returned.reshape(outkinds, experts, GROUP, capacity, width).astyp...]
  transfers between devices with their start and end apart: 6 -> 0, of which waited for: 4 -> 0; matrix products, arithmetic and copies ran while one was open for 18% -> 0% of each run, Pallas kernels for 0% -> 0%
where the time goes in v1:
time: 102 us; the launch traced here: 101 us
  Pallas kernels  95.8 us (94%)
  local copies, waits for them, and re-layouts  4.28 us (4%)
    pallas_call x1, Pallas kernels, body(): pl.pallas_call(functools.partial(kernel, experts, cap, slot, chunks), out...  95.8 us
    unnamed x12, local copies, waits for them, and re-layouts  3.61 us

profile of v1, /device:TPU:0, one launch (start us, length us, event | category | flops | bytes accessed | tf_op | source)
XLA Modules:
  0.0 101.3 jit_solution(4051226055730494492)
XLA Ops:
  0.6 0.0 copy-start.4
  0.6 0.0 copy-start.3
  0.6 0.7 copy-done.4
  1.3 0.0 copy-done.3
  1.3 0.0 copy-start.2
  1.3 0.0 copy-start.1
  1.3 0.7 copy-done.2
  2.0 0.0 copy-done.1
  2.0 0.6 fusion
  2.6 0.7 copy.12.info
  3.3 95.8 %shard_map.113 = (bf16[16,3584]{1,0:T(8,128)(2,1)}, bf16[16,3584]{1,0:T(8,128)(2,1)}) custom-call(f32[16,8]{1,0:T(8,128)} %copy.12.info, f32[8,16]{1,0:T(8,128)} %get-tuple-element.6.info_t, bf16[16,3584]{1,0:T(8,128)(2,1)} %bitcast.21, bf16[16,3584]{1,0:T(8,128)(2,1)} %bitcast.22, bf16[16,3584]{1,0:T(8,128)(2,1)} %bitcast.23, bf16[3584,128]{1,0:T(8,128)(2,1)} %bitcast.16, ...), custom_call_target="tpu_custom_call" | custom-call | tf_op jit(solution)/shard_map/pallas_call | solution.py:313
  99.1 0.0 copy-start
  99.1 1.6 %copy.15 = bf16[1,16,3584]{2,1,0:T(8,128)(2,1)} copy(bf16[1,16,3584]{2,1,0:T(8,128)(2,1)} %bitcast.20) | data formatting | bytes 229376
  100.7 0.0 copy-done
  100.7 0.6 copy.16
  (1 shorter events, 0.0 us)
Async XLA Ops:
  0.6 0.7 copy-start.4
  0.6 0.7 copy-start.3
  1.3 0.7 copy-start.2
  1.3 0.7 copy-start.1
  99.1 1.6 %copy-start = (bf16[16,3584]{1,0:T(8,128)(2,1)S(1)}, bf16[16,3584]{1,0:T(8,128)(2,1)}, u32[]{:S(2)}) copy-start(bf16[16,3584]{1,0:T(8,128)(2,1)} %get-tuple-element.5) | copy-start | bytes 344068

commit v2 on v1

--- a/solution.py
+++ b/solution.py
@@ -8,7 +8,7 @@
 from jax.sharding import PartitionSpec as P
 
 GROUP = 8
-CHUNKS = 4
+CHUNKS = 7
 F32 = jnp.float32
 BF16 = jnp.bfloat16
 
@@ -33,7 +33,7 @@
 def kernel(
     experts, cap, slot, chunks,
     info, info_t, tok_f, tok_b, grad, wg, wu, wd, y_ref, dx_ref,
-    bundles, gathered, acc, hidden, away, near, from_pair, summed, diag, relay,
+    bundles, gathered, acc, w_in, w_out, hidden, away, near, from_pair, summed, diag, relay,
     from_x, from_y, back, home,
     z_s, z_r, own_s, own_r, dia_s, dia_r, pair_s, pair_r,
     op_s, op_r, dg_s, dg_r, x_s, x_r, y_s, y_r, b_s, b_r,
@@ -57,16 +57,19 @@
     def z_copy(c, d):
         return copy(bundles.at[c, d], gathered.at[c, 0, d], z_s.at[c, d], z_r.at[c, d], planes[d])
 
-    def own_copy(c, k):
-        return copy(gathered.at[c, 0], gathered.at[c, k], own_s.at[c, k], own_r.at[c, k],
+    def piece(c, k, part):
+        return gathered.at[c, k]
+
+    def own_copy(c, p, k):
+        return copy(piece(c, 0, p), piece(c, k, p), own_s.at[c, p, k], own_r.at[c, p, k],
                     chip_x if k == 1 else chip_y)
 
-    def dia_copy(c):
+    def dia_copy(c, p):
         k, target = (1, chip_y) if c % 2 == 0 else (2, chip_x)
-        return copy(gathered.at[c, k], gathered.at[c, 3], dia_s.at[c], dia_r.at[c], target)
-
-    def pair_copy(c, k):
-        return copy(gathered.at[c, k], gathered.at[c, 4 + k], pair_s.at[c, k], pair_r.at[c, k], pair)
+        return copy(piece(c, k, p), piece(c, 3, p), dia_s.at[c, p], dia_r.at[c, p], target)
+
+    def pair_copy(c, p, k):
+        return copy(piece(c, k, p), piece(c, 4 + k, p), pair_s.at[c, p, k], pair_r.at[c, p, k], pair)
 
     def op_copy(c):
         return copy(away.at[c], from_pair.at[c], op_s.at[c], op_r.at[c], pair)
@@ -135,55 +138,74 @@
     last = (rest - middle.astype(F32)).astype(BF16)
     join = jnp.concatenate([high, middle, last, join_b.astype(BF16)], axis=0)
 
+    def send_own(c, p):
+        own_copy(c, p, 1).start()
+        own_copy(c, p, 2).start()
+        pair_copy(c, p, 0).start()
+
     pl.semaphore_wait(barrier, len(friends))
     for c in range(chunks):
         at = slice(c * cols, (c + 1) * cols)
         block = nn(pick_f, tok_f[:, at]) + nn(pick_x, tok_b[:, at]) + gain * nn(pick_g, grad[:, at])
         block = block.astype(BF16).reshape(experts, slot, cols)
-        gathered[c, 0, 0] = block[0]
         for d in range(1, experts):
             bundles[c, d] = block[d]
             z_copy(c, d).start()
+        gathered[c, 0, 0] = block[0]
 
     acc[...] = jnp.zeros_like(acc)
 
+    corner0 = lax.broadcasted_iota(jnp.int32, (128, 128), 0)
+    corner1 = lax.broadcasted_iota(jnp.int32, (128, 128), 1)
+    eye = (corner0 == corner1).astype(F32).astype(BF16)
+
     def gather_own(c):
+        at = slice(c * cols, (c + 1) * cols)
+        w_in[c, :, 0:128] = wg[at, :]
+        w_in[c, :, 128:256] = wu[at, :]
+        w_out[c, 0:128, :] = wd[:, at]
+        w_out[c, 128:256, :] = nt(eye, wg[at, :]).astype(BF16)
+        w_out[c, 256:384, :] = nt(eye, wu[at, :]).astype(BF16)
         for d in range(1, experts):
             z_copy(c, d).wait_recv()
-        own_copy(c, 1).start()
-        own_copy(c, 2).start()
-        pair_copy(c, 0).start()
-
-    def gather_next(c):
+        send_own(c, 1)
+
+    def gather_next(c, p):
         order = (1, 2) if c % 2 == 0 else (2, 1)
-        own_copy(c, order[0]).wait_recv()
-        dia_copy(c).start()
-        pair_copy(c, order[0]).start()
-        own_copy(c, order[1]).wait_recv()
-        pair_copy(c, order[1]).start()
-
-    def gather_last(c):
-        dia_copy(c).wait_recv()
-        pair_copy(c, 3).start()
+        own_copy(c, p, order[0]).wait_recv()
+        dia_copy(c, p).start()
+        pair_copy(c, p, order[0]).start()
+        own_copy(c, p, order[1]).wait_recv()
+        pair_copy(c, p, order[1]).start()
+
+    def gather_last(c, p):
+        dia_copy(c, p).wait_recv()
+        pair_copy(c, p, 3).start()
 
     def multiply(c):
-        for k in range(4):
-            pair_copy(c, k).wait_recv()
+        for p in (1,):
+            for k in range(4):
+                pair_copy(c, p, k).wait_recv()
         at = slice(c * cols, (c + 1) * cols)
 
-        def one(q, carry):
-            part = gathered[c, q].reshape(rows, cols)
-            acc[q, :, 0:128] += nn(part, wg[at, :])
-            acc[q, :, 128:256] += nn(part, wu[at, :])
-            acc[q, :, 256:384] += nt(part, wd[:, at])
+        def one(h, carry):
+            half = pl.ds(4 * h, 4)
+            part = gathered[c, half].reshape(4 * rows, cols)
+            acc[half, :, 0:256] += nn(part, w_in[c]).reshape(4, rows, 256)
+            acc[half, :, 256:384] += nt(part, wd[:, at]).reshape(4, rows, 128)
             return carry
 
-        lax.fori_loop(0, 8, one, 0)
+        lax.fori_loop(0, 2, one, 0)
 
     for step in range(chunks + 3):
-        for lag, stage in enumerate((gather_own, gather_next, gather_last, multiply)):
-            if 0 <= step - lag < chunks:
-                stage(step - lag)
+        if step < chunks:
+            gather_own(step)
+        if 0 <= step - 1 < chunks:
+            gather_next(step - 1, 1)
+        if 0 <= step - 2 < chunks:
+            gather_last(step - 2, 1)
+        if 0 <= step - 3:
+            multiply(step - 3)
 
     out_i = lax.broadcasted_iota(jnp.int32, (outs, rows), 0)
     in_i = lax.broadcasted_iota(jnp.int32, (outs, rows), 1)
@@ -215,24 +237,13 @@
     lax.fori_loop(0, 8, activate, 0)
 
     def partial(q, c):
-        at = slice(c * cols, (c + 1) * cols)
-        total = nn(hidden[q, :, 0:128], wd[:, at])
-        total = total + nt(hidden[q, :, 128:256], wg[at, :])
-        total = total + nt(hidden[q, :, 256:384], wu[at, :])
-        return total.astype(BF16)
+        total = nn(hidden[q:q + 4].reshape(4 * outs, 384), w_out[c])
+        return total.astype(BF16).reshape(4, outs, cols)
 
     def produce(c):
-        def far(r, carry):
-            away[c, r] = partial(4 + r, c)
-            return carry
-
-        def close(r, carry):
-            near[c, r] = partial(r, c)
-            return carry
-
-        lax.fori_loop(0, 4, far, 0)
+        away[c] = partial(4, c)
         op_copy(c).start()
-        lax.fori_loop(0, 4, close, 0)
+        near[c] = partial(0, c)
 
     def chip_sum(c):
         op_copy(c).wait_recv()
@@ -285,11 +296,13 @@
         for d in range(1, experts):
             z_copy(c, d).wait_send()
             b_copy(c, d).wait_send()
-        for k in (1, 2):
-            own_copy(c, k).wait_send()
-        for k in range(4):
-            pair_copy(c, k).wait_send()
-        for made in (dia_copy, op_copy, dg_copy, x_copy, y_copy):
+        for p in (1,):
+            for k in (1, 2):
+                own_copy(c, p, k).wait_send()
+            for k in range(4):
+                pair_copy(c, p, k).wait_send()
+            dia_copy(c, p).wait_send()
+        for made in (op_copy, dg_copy, x_copy, y_copy):
             made(c).wait_send()
 
 
@@ -319,6 +332,8 @@
             vmem(chunks, experts, slot, cols),
             vmem(chunks, 8, experts, slot, cols),
             pltpu.VMEM((8, rows, 384), F32),
+            vmem(chunks, cols, 256),
+            vmem(chunks, 384, cols),
             vmem(8, outs, 384),
             vmem(chunks, 4, outs, cols),
             vmem(chunks, 4, outs, cols),
@@ -331,9 +346,9 @@
             vmem(chunks, experts, slot, cols),
             vmem(chunks, experts, slot, cols),
             dma((chunks, experts)), dma((chunks, experts)),
-            dma((chunks, 3)), dma((chunks, 3)),
-            dma((chunks,)), dma((chunks,)),
-            dma((chunks, 4)), dma((chunks, 4)),
+            dma((chunks, 2, 3)), dma((chunks, 2, 3)),
+            dma((chunks, 2)), dma((chunks, 2)),
+            dma((chunks, 2, 4)), dma((chunks, 2, 4)),
             dma((chunks,)), dma((chunks,)),
             dma((chunks,)), dma((chunks,)),
             dma((chunks,)), dma((chunks,)),

time: 102 us -> 95.2 us (0.933)
  Pallas kernels: 95.8 us -> 89.4 us
    pallas_call x1, Pallas kernels: 95.8 us -> 89.4 us  [body(): pl.pallas_call(functools.partial(kernel, experts, cap, slot, chunks), out...]
where the time goes in v2:
time: 95.2 us; the launch traced here: 95 us
  Pallas kernels  89.4 us (94%)
  local copies, waits for them, and re-layouts  4.28 us (4%)
    pallas_call x1, Pallas kernels, body(): pl.pallas_call(functools.partial(kernel, experts, cap, slot, chunks), out...  89.4 us
    unnamed x12, local copies, waits for them, and re-layouts  3.61 us

profile of v2, /device:TPU:0, one launch (start us, length us, event | category | flops | bytes accessed | tf_op | source)
XLA Modules:
  0.0 95.0 jit_solution(10897515001552326793)
XLA Ops:
  0.6 0.0 copy-start.4
  0.6 0.0 copy-start.3
  0.6 0.7 copy-done.4
  1.3 0.0 copy-done.3
  1.3 0.0 copy-start.2
  1.3 0.0 copy-start.1
  1.3 0.7 copy-done.2
  2.0 0.0 copy-done.1
  2.0 0.6 fusion
  2.6 0.7 copy.12.info
  3.3 89.4 %shard_map.113 = (bf16[16,3584]{1,0:T(8,128)(2,1)}, bf16[16,3584]{1,0:T(8,128)(2,1)}) custom-call(f32[16,8]{1,0:T(8,128)} %copy.12.info, f32[8,16]{1,0:T(8,128)} %get-tuple-element.6.info_t, bf16[16,3584]{1,0:T(8,128)(2,1)} %bitcast.21, bf16[16,3584]{1,0:T(8,128)(2,1)} %bitcast.22, bf16[16,3584]{1,0:T(8,128)(2,1)} %bitcast.23, bf16[3584,128]{1,0:T(8,128)(2,1)} %bitcast.16, ...), custom_call_target="tpu_custom_call" | custom-call | tf_op jit(solution)/shard_map/pallas_call | solution.py:326
  92.8 0.0 copy-start
  92.8 1.6 %copy.15 = bf16[1,16,3584]{2,1,0:T(8,128)(2,1)} copy(bf16[1,16,3584]{2,1,0:T(8,128)(2,1)} %bitcast.20) | data formatting | bytes 229376
  94.3 0.0 copy-done
  94.4 0.6 copy.16
  (1 shorter events, 0.0 us)
Async XLA Ops:
  0.6 0.7 copy-start.4
  0.6 0.7 copy-start.3
  1.3 0.7 copy-start.2
  1.3 0.7 copy-start.1
  92.8 1.6 %copy-start = (bf16[16,3584]{1,0:T(8,128)(2,1)S(1)}, bf16[16,3584]{1,0:T(8,128)(2,1)}, u32[]{:S(2)}) copy-start(bf16[16,3584]{1,0:T(8,128)(2,1)} %get-tuple-element.5) | copy-start | bytes 344068
